TPU v7x, 32 devices: a whole 2x2x4 slice. The times are simulated.
32 devices in a mesh: seq: 8 (over y, x, core), head: 4 (over z).
Axes of the slice: x: 2, y: 2, z: 4, core: 2. Of those that a mesh axis runs over, the one named last changes fastest.
Arguments:
- queries: bfloat16 [2, 2048, 20, 128], P(None, ('seq', 'head')), may hold values from -96 to 96
- grad_out: bfloat16 [2, 2048, 20, 128], P(None, ('seq', 'head')), may hold values from -6 to 6
- keys: bfloat16 [2048, 4, 128], P('seq', 'head'), may hold values from -6 to 6
- values: bfloat16 [2048, 4, 128], P('seq', 'head'), may hold values from -6 to 6
- doc_start: int32 [2048], replicated, may hold values from 0 to 2047, as said below
Outputs:
- query_grads: bfloat16 [2, 2048, 20, 128], P(None, ('seq', 'head'))
- key_grads: bfloat16 [2048, 4, 128], P('seq', 'head')
- value_grads: bfloat16 [2048, 4, 128], P('seq', 'head')
Inputs may be any that keep to these rules, and one draw needn't show every extreme that they name: doc_start[i] is the first position of token i's document, so doc_start[i] <= i; it is 0 for every token before position 1024, at most four documents begin at or after it, and the last token begins a document of its own.
All inputs are finite; a program needn't handle non-finite values.
Results may differ from a plain program's by a relative error of at most 0.005.
Values may be sent and summed in bfloat16 or wider, within the bound.
No kernel may reach another device: no remote copies, remote signals or barrier semaphores. Data moves between devices by JAX's collectives and lax.ppermute only.
A program may use at most 128 MiB of HBM per device.

v0:
```python
import math

import jax
import jax.numpy as jnp
from jax import lax
from jax.sharding import PartitionSpec as P

NEG_START = -1e30


def block_length(key_count):
    return math.gcd(key_count, 1024)


def over_blocks(advance, carried, pieces):
    key_count = pieces[0].shape[0]
    block_rows = block_length(key_count)

    def one_block(block_index, inner):
        block_start = block_index * block_rows
        sliced = tuple(
            (
                lax.dynamic_slice_in_dim(piece_rows, block_start, block_rows, 0)
                for piece_rows in pieces
            )
        )
        return advance(inner, sliced, block_start)

    return lax.fori_loop(0, key_count // block_rows, one_block, carried)


def masked_scores(group, key_block, key_start, score_scale):
    query_rows, grad_rows, starts, positions = group
    key_pos = key_start + jnp.arange(key_block.shape[0], dtype=jnp.int32)
    allowed = (key_pos[None, :] >= starts[:, None]) & (key_pos[None, :] <= positions[:, None])
    scores = (
        jnp.einsum("lrkgd,nkd->lkgrn", query_rows, key_block, preferred_element_type=jnp.float32)
        * score_scale
    )
    return jnp.where(allowed, scores, -jnp.inf)


def stats_update(group, carried, key_block, value_block, key_start, score_scale):

    def stats_compute(inner):
        row_max, row_sum, weighted = inner
        scores = masked_scores(group, key_block, key_start, score_scale)
        new_max = jnp.maximum(row_max, jnp.max(scores, axis=-1))
        raw_weights = jnp.exp(scores - new_max[..., None])
        grad_probs = jnp.einsum(
            "lrkgd,nkd->lkgrn", group[1], value_block, preferred_element_type=jnp.float32
        )
        rescale = jnp.exp(row_max - new_max)
        return (
            new_max,
            row_sum * rescale + jnp.sum(raw_weights, axis=-1),
            weighted * rescale + jnp.sum(raw_weights * grad_probs, axis=-1),
        )

    return lax.cond(key_start > jnp.max(group[3]), lambda inner: inner, stats_compute, carried)


def grads_update(group, row_stats, carried, key_block, value_block, key_start, score_scale):
    log_norm, row_delta = row_stats

    def grads_compute(inner):
        query_acc, key_buffer, value_buffer = inner
        scores = masked_scores(group, key_block, key_start, score_scale)
        prob_rows = jnp.exp(scores - log_norm[..., None])
        grad_probs = jnp.einsum(
            "lrkgd,nkd->lkgrn", group[1], value_block, preferred_element_type=jnp.float32
        )
        grad_scores = prob_rows * (grad_probs - row_delta[..., None])
        grad_low = grad_scores.astype(jnp.bfloat16)
        prob_low = prob_rows.astype(jnp.bfloat16)
        query_acc = query_acc + jnp.einsum(
            "lkgrn,nkd->lrkgd", grad_low, key_block, preferred_element_type=jnp.float32
        )
        key_part = jnp.einsum(
            "lkgrn,lrkgd->nkd", grad_low, group[0], preferred_element_type=jnp.float32
        )
        value_part = jnp.einsum(
            "lkgrn,lrkgd->nkd", prob_low, group[1], preferred_element_type=jnp.float32
        )
        block_rows = key_block.shape[0]
        key_buffer = lax.dynamic_update_slice_in_dim(
            key_buffer,
            lax.dynamic_slice_in_dim(key_buffer, key_start, block_rows, 0) + key_part,
            key_start,
            0,
        )
        value_buffer = lax.dynamic_update_slice_in_dim(
            value_buffer,
            lax.dynamic_slice_in_dim(value_buffer, key_start, block_rows, 0) + value_part,
            key_start,
            0,
        )
        return (query_acc, key_buffer, value_buffer)

    return lax.cond(key_start > jnp.max(group[3]), lambda inner: inner, grads_compute, carried)


def layer_pass(groups, keys, values, score_scale, total_rows):
    stat_init = []
    for group in groups:
        layer_count, row_count, key_heads, group_size, head_width = group[0].shape
        stat_shape = (layer_count, key_heads, group_size, row_count)
        stat_init.append(
            (
                jnp.full(stat_shape, NEG_START, jnp.float32),
                jnp.zeros(stat_shape, jnp.float32),
                jnp.zeros(stat_shape, jnp.float32),
            )
        )

    def advance(inner, sliced, key_start):
        return tuple(
            (
                stats_update(group, member, sliced[0], sliced[1], key_start, score_scale)
                for group, member in zip(groups, inner)
            )
        )

    gathered_stats = over_blocks(
        advance,
        tuple(stat_init),
        (
            lax.all_gather(keys, "seq", axis=0, tiled=True),
            lax.all_gather(values, "seq", axis=0, tiled=True),
        ),
    )
    row_stats = tuple(
        ((member[0] + jnp.log(member[1]), member[2] / member[1]) for member in gathered_stats)
    )
    buffer_shape = (total_rows, keys.shape[1], keys.shape[2])
    grad_init = (
        tuple((jnp.zeros(group[0].shape, jnp.float32) for group in groups)),
        jnp.zeros(buffer_shape, jnp.float32),
        jnp.zeros(buffer_shape, jnp.float32),
    )

    def advance(inner, sliced, key_start):
        query_accs, key_buffer, value_buffer = inner
        updated = []
        for group, stats_pair, query_acc in zip(groups, row_stats, query_accs):
            query_acc, key_buffer, value_buffer = grads_update(
                group,
                stats_pair,
                (query_acc, key_buffer, value_buffer),
                sliced[0],
                sliced[1],
                key_start,
                score_scale,
            )
            updated.append(query_acc)
        return (tuple(updated), key_buffer, value_buffer)

    query_accs, key_buffer, value_buffer = over_blocks(
        advance,
        grad_init,
        (
            lax.all_gather(keys, "seq", axis=0, tiled=True),
            lax.all_gather(values, "seq", axis=0, tiled=True),
        ),
    )
    key_own, value_own = (
        lax.psum_scatter(key_buffer, "seq", scatter_dimension=0, tiled=True),
        lax.psum_scatter(value_buffer, "seq", scatter_dimension=0, tiled=True),
    )
    return (query_accs, key_own, value_own)


def per_device(queries, grad_out, keys, values, doc_start):
    layer_count = queries.shape[0]
    head_width = queries.shape[3]
    key_heads = keys.shape[1]
    score_scale = 1.0 / math.sqrt(head_width)
    regrouped, regrads = (
        lax.all_to_all(queries, "head", split_axis=2, concat_axis=1, tiled=True),
        lax.all_to_all(grad_out, "head", split_axis=2, concat_axis=1, tiled=True),
    )
    row_count = regrouped.shape[1]
    local_heads = regrouped.shape[2]
    group_size = local_heads // key_heads
    five_shape = (layer_count, row_count, key_heads, group_size, head_width)
    query_rows = regrouped.reshape(five_shape)
    grad_rows = regrads.reshape(five_shape)
    seq_index = lax.axis_index("seq")
    seq_count = lax.axis_size("seq")
    total_rows = row_count * seq_count
    offsets = jnp.arange(row_count, dtype=jnp.int32)
    own_pos = seq_index * row_count + offsets
    own_start = lax.dynamic_slice_in_dim(doc_start, seq_index * row_count, row_count, 0)
    groups = ((query_rows, grad_rows, own_start, own_pos),)
    query_accs, key_total, value_total = layer_pass(groups, keys, values, score_scale, total_rows)
    query_low = tuple(((acc * score_scale).astype(jnp.bfloat16) for acc in query_accs))
    query_final = query_low[0]
    query_final = query_final.reshape(layer_count, row_count, local_heads, head_width)
    query_grads = lax.all_to_all(query_final, "head", split_axis=1, concat_axis=2, tiled=True)
    key_grads = (key_total * score_scale).astype(jnp.bfloat16)
    value_grads = value_total.astype(jnp.bfloat16)
    return (query_grads, key_grads, value_grads)


def solution(mesh):
    in_specs = (
        P(None, ("seq", "head"), None, None),
        P(None, ("seq", "head"), None, None),
        P("seq", "head", None),
        P("seq", "head", None),
        P(),
    )
    out_specs = (
        P(None, ("seq", "head"), None, None),
        P("seq", "head", None),
        P("seq", "head", None),
    )
    return jax.shard_map(
        per_device, mesh=mesh, in_specs=in_specs, out_specs=out_specs, check_vma=False
    )
```

profile of v0, /device:TPU:0, one launch (start us, length us, event | category | flops | bytes accessed | tf_op | source)
XLA Modules:
  0.0 185.2 jit_solution(4369030967913682128)
XLA Ops:
  7.2 2.0 %copy.78 = bf16[2,64,20,128]{3,1,0,2:T(8,128)(2,1)} copy(bf16[2,64,20,128]{3,1,2,0:T(8,128)(2,1)} %param.13) | data formatting | bytes 1310720 | tf_op args[0]
  9.1 6.3 %all-to-all-start = ((bf16[2,64,20,128]{3,1,0,2:T(8,128)(2,1)}), bf16[2,64,20,128]{3,1,0,2:T(8,128)(2,1)S(1)}, u32[]{:S(2)}, u32[]{:S(2)}) async-start(bf16[2,64,20,128]{3,1,0,2:T(8,128)(2,1)} %copy.78), calls=%async_computation | async-start | bytes 1310720 | tf_op jit(solution)/shard_map/all_to_all | solution.py:179
  15.5 2.0 %copy.80 = bf16[2,64,20,128]{3,1,0,2:T(8,128)(2,1)} copy(bf16[2,64,20,128]{3,1,2,0:T(8,128)(2,1)} %param.14) | data formatting | bytes 1310720 | tf_op args[1]
  17.4 15.3 %all-to-all-done = bf16[2,64,20,128]{3,1,0,2:T(8,128)(2,1)S(1)} async-done(((bf16[2,64,20,128]{3,1,0,2:T(8,128)(2,1)}), bf16[2,64,20,128]{3,1,0,2:T(8,128)(2,1)S(1)}, u32[]{:S(2)}, u32[]{:S(2)}) %all-to-all-start) | async-done | bytes 655392 | tf_op jit(solution)/shard_map/all_to_all | solution.py:179
  32.8 3.5 %all-to-all-start.1 = ((bf16[2,64,20,128]{3,1,0,2:T(8,128)(2,1)}), bf16[2,64,20,128]{3,1,0,2:T(8,128)(2,1)S(1)}, u32[]{:S(2)}, u32[]{:S(2)}) async-start(bf16[2,64,20,128]{3,1,0,2:T(8,128)(2,1)} %copy.80), calls=%async_computation.1 | async-start | bytes 1310720 | tf_op jit(solution)/shard_map/all_to_all | solution.py:180
  36.3 0.0 reduce-scatter.5.cloned.1.call-start
  36.3 0.7 add_reduce_fusion
  37.0 0.8 dynamic_slice.71
  37.8 10.1 %all_gather.8 = bf16[2048,1,128]{2,0,1:T(8,128)(2,1)S(1)} all-gather(bf16[256,1,128]{2,0,1:T(8,128)(2,1)} %param.15), channel_id=1, replica_groups=mesh['seq'=8,'head'=4] {'seq'}, dimensions={0}, use_global_device_ids=true | all-gather | bytes 589824 | tf_op jit(solution)/shard_map/all_gather | solution.py:162
  47.9 10.8 %all_gather.9 = bf16[2048,1,128]{2,0,1:T(8,128)(2,1)} all-gather(bf16[256,1,128]{2,0,1:T(8,128)(2,1)} %param.16), channel_id=1, replica_groups=mesh['seq'=8,'head'=4] {'seq'}, dimensions={0}, use_global_device_ids=true | all-gather | bytes 589824 | tf_op jit(solution)/shard_map/all_gather | solution.py:163
  58.8 0.0 all-to-all-done.1
  58.8 0.1 copy.81
  58.9 0.0 copy-start.3
  59.0 0.8 copy-done.3
  59.7 8.9 %while.38 = (s32[]{:T(128)}, f32[2,1,5,256]{3,2,0,1:T(8,128)S(1)}, f32[2,1,5,256]{3,2,0,1:T(8,128)S(1)}, f32[2,1,5,256]{3,2,0,1:T(8,128)S(1)}, s32[]{:T(128)}, /...) while((s32[]{:T(128)}, f32[2,1,5,256]{3,2,0,1:T(8,128)S(1)}, ...), condition=%wide.region_7.8_spmd.clone, body=%wide.region_1.7_spmd.clone.sunk | while | flops 1374429952 | bytes 36642160 | solution.py:29
  60.4 7.4 %conditional.6 = (f32[2,1,5,256]{3,2,0,1:T(8,128)S(1)}, f32[2,1,5,256]{3,2,0,1:T(8,128)S(1)}, f32[2,1,5,256]{3,2,0,1:T(8,128)S(1)}) conditional(s32[]{:T(128)} %convert_element_type.56, (s32[]{:T(128)}, s32[256]{0:T(256)S(1)}, s32[]{:T(128)}, bf16[2048,1,128]{2,0,1:T(8,128)(2,1)S(1)}, bf16[2,256,1,5,128]{4,1,3,0,2:T(8,128)(2,1)S(1)}, ...), branch_computations={%region_2.5_spmd, %region_6.6_spmd} | conditional | flops 1374429952 | bytes 36620392 | solution.py:60
  60.4 0.0 copy-start.5
  60.5 0.3 compare_and_fusion
  60.8 1.6 fusion.6
  62.4 0.0 copy-done.5
  62.4 3.2 %fusion.4 = f32[2,5,256]{2,1,0:T(8,128)S(1)} fusion(f32[1024,2,256,5]{2,0,3,1:T(8,128)S(1)} %get-tuple-element.948, f32[2,5,256]{2,1,0:T(8,128)S(1)} %bitcast.164, pred[256,1024]{0,1:T(8,128)(4,1)S(1)} %compare_and_fusion, bf16[2,256,1,5,128]{4,1,3,0,2:T(8,128)(2,1)S(1)} %get-tuple-element.705, bf16[2048,1,128]{2,0,1:T(8,128)(2,1)S(1)} %copy-done.5, ...), kind=kOutput, calls=%fused_computation.3 | convolution fusion | flops 684193280 | bytes 11692036 | tf_op jit(solution)/shard_map/while/body/eval_jaxpr/cond/branch_0_fun/lrkgd,nkd->lkgrn/dot_general | solution.py:50
  65.6 2.1 %fusion.5 = f32[2,5,256]{2,1,0:T(8,128)S(1)} fusion(f32[1024,2,256,5]{2,0,3,1:T(8,128)S(1)} %get-tuple-element.948, f32[2,5,256]{2,1,0:T(8,128)S(1)} %bitcast.165, pred[256,1024]{0,1:T(8,128)(4,1)S(1)} %compare_and_fusion), kind=kLoop, calls=%fused_computation.6 | loop fusion | flops 10483200 | bytes 10768384 | tf_op jit(solution)/shard_map/while/body/eval_jaxpr/cond/branch_0_fun/reduce_sum | solution.py:56
  68.6 0.6 fusion.61
  69.2 0.1 broadcast.47.clone
  69.3 1.0 broadcast.47
  70.3 0.1 broadcast_in_dim.43
  70.4 11.9 %while.39 = (s32[]{:T(128)}, f32[2,256,1,5,128]{1,4,3,0,2:T(8,128)S(1)}, f32[2048,1,128]{2,0,1:T(8,128)}, f32[2048,1,128]{2,0,1:T(8,128)S(1)}, s32[]{:T(128)}, /...) while((s32[]{:T(128)}, ...), condition=%wide.region_11.0_spmd.clone, body=%wide.region_8.11_spmd.clone.sunk | while | flops 3383035136 | bytes 69350960 | solution.py:29
  71.3 10.3 %conditional.7 = ((f32[2,256,1,5,128]{1,4,3,0,2:T(8,128)S(1)}, f32[2048,1,128]{2,0,1:T(8,128)}, f32[2048,1,128]{2,0,1:T(8,128)S(1)})) conditional(s32[]{:T(128)} %convert_element_type.57, (s32[]{:T(128)}, bf16[2048,1,128]{2,0,1:T(8,128)(2,1)S(1)}, s32[256]{0:T(256)S(1)}, s32[]{:T(128)}, bf16[2,256,1,5,128]{4,1,0,3,2:T(8,128)(2,1)S(1)}, ...), branch_computations={%region_9.9_spmd, %region_10.10_spmd} | conditional | flops 3383035136 | bytes 69349640 | solution.py:100
  71.4 0.0 copy-start.4
  71.4 0.0 copy-start.8
  71.4 0.3 compare_and_fusion.1
  71.7 1.5 fusion.47
  73.2 0.0 copy-done.4
  73.2 0.0 copy-done.8
  73.2 0.0 copy-start.6
  73.2 0.0 copy-start.7
  73.3 2.4 %fusion.37 = f32[2048,1,128]{2,0,1:T(8,128)S(1)} fusion(f32[2048,1,128]{2,0,1:T(8,128)S(1)} %get-tuple-element.732, s32[]{:T(128)S(6)} %select_n.43, bf16[2,256,1,5,128]{4,1,0,3,2:T(8,128)(2,1)S(1)} %copy-done.4, f32[1024,2,256,5]{2,0,3,1:T(8,128)S(1)} %fusion.47, f32[2,5,256]{2,1,0:T(8,128)S(1)} %bitcast.173, pred[256,1024]{0,1:T(8,128)(4,1)S(1)} %compare_and_fusion.1), kind=kOutput, calls=%fused_computation.42 | convolution fusion | flops 681705472 | bytes 12468228 | tf_op jit(solution)/shard_map/while/body/eval_jaxpr/cond/branch_0_fun/lkgrn,lrkgd->nkd/dot_general | solution.py:82
  75.7 0.0 copy-done.6
  75.7 0.0 copy-done.7
  75.7 0.0 copy-start.1
  75.7 3.3 %fusion.22 = bf16[2,5,256,1024]{2,3,1,0:T(8,128)(2,1)S(1)} fusion(f32[1024,2,256,5]{2,0,3,1:T(8,128)S(1)} %fusion.47, f32[2,5,256]{2,1,0:T(8,128)S(1)} %bitcast.172, f32[2,5,256]{2,1,0:T(8,128)S(1)} %bitcast.174, pred[256,1024]{0,1:T(8,128)(4,1)S(1)} %compare_and_fusion.1, bf16[2048,1,128]{2,0,1:T(8,128)(2,1)S(1)} %copy-done.6, s32[]{:T(128)S(6)} %select_n.43, ...), kind=kOutput, calls=%fused_computation.32 | convolution fusion | flops 686817280 | bytes 16941060 | tf_op jit(solution)/shard_map/while/body/eval_jaxpr/cond/branch_0_fun/lrkgd,nkd->lkgrn/dot_general | solution.py:70
  79.1 0.0 copy-done.1
  79.1 1.5 fusion.43
  80.6 0.0 copy-start.2
  80.6 1.0 fusion.27
  81.6 0.0 copy-done.2
  82.4 0.0 copy-start
  82.4 1.0 copy-done
  83.4 0.0 reduce-scatter.5.cloned.1.call-update
  83.4 0.0 reduce-scatter.3.cloned.1.call-start
  83.5 0.7 reduce-scatter.3.cloned.1.call-update
  84.2 0.4 copy.84
  84.6 0.2 fusion.60
  84.7 0.7 copy.85
  85.4 22.6 %all_to_all.48 = bf16[2,256,5,128]{3,0,2,1:T(2,128)(2,1)S(1)} all-to-all(bf16[2,256,5,128]{3,0,2,1:T(2,128)(2,1)S(1)} %copy.85), channel_id=1, replica_groups=mesh['seq'=8,'head'=4] {'head'}, dimensions={1} | all-to-all | bytes 1310720 | tf_op jit(solution)/shard_map/all_to_all | solution.py:199
  108.0 0.1 copy.86
  108.1 0.9 copy.87
  109.0 28.6 %reduce-scatter.5.cloned.1.call-done = f32[256,1,128]{2,0,1:T(8,128)} async-done(((f32[2048,1,128]{2,0,1:T(8,128)}), f32[256,1,128]{2,0,1:T(8,128)}) %reduce-scatter.5.cloned.1.call-update) | async-done | bytes 131088 | tf_op jit(solution)/shard_map/reduce_scatter | solution.py:168
  137.6 1.5 convert_element_type.39
  139.2 37.7 %reduce-scatter.3.cloned.1.call-done = f32[256,1,128]{2,0,1:T(8,128)} async-done(((f32[2048,1,128]{2,0,1:T(8,128)}), f32[256,1,128]{2,0,1:T(8,128)}) %reduce-scatter.3.cloned.1.call-update) | async-done | bytes 131088 | tf_op jit(solution)/shard_map/reduce_scatter | solution.py:167
  176.8 1.5 multiply_convert_fusion.1
  (21 shorter events, 0.3 us)
Async XLA Ops:
  9.1 23.6 %all-to-all-start = ((bf16[2,64,20,128]{3,1,0,2:T(8,128)(2,1)}), bf16[2,64,20,128]{3,1,0,2:T(8,128)(2,1)S(1)}, u32[]{:S(2)}, u32[]{:S(2)}) async-start(bf16[2,64,20,128]{3,1,0,2:T(8,128)(2,1)} %copy.78), calls=%async_computation | async-start | bytes 1310720 | tf_op jit(solution)/shard_map/all_to_all | solution.py:179
  32.8 26.0 %all-to-all-start.1 = ((bf16[2,64,20,128]{3,1,0,2:T(8,128)(2,1)}), bf16[2,64,20,128]{3,1,0,2:T(8,128)(2,1)S(1)}, u32[]{:S(2)}, u32[]{:S(2)}) async-start(bf16[2,64,20,128]{3,1,0,2:T(8,128)(2,1)} %copy.80), calls=%async_computation.1 | async-start | bytes 1310720 | tf_op jit(solution)/shard_map/all_to_all | solution.py:180
  36.3 101.4 %reduce-scatter.5.cloned.1.call-start = ((), (), s32[]{:S(2)}) async-start(), calls=%async_computation.6 | async-start | bytes 1179648 | tf_op jit(solution)/shard_map/reduce_scatter | solution.py:168
  58.9 0.8 copy-start.3
  60.4 1.9 %copy-start.5 = (bf16[2048,1,128]{2,0,1:T(8,128)(2,1)S(1)}, bf16[2048,1,128]{2,0,1:T(8,128)(2,1)}, u32[]{:S(2)}) copy-start(bf16[2048,1,128]{2,0,1:T(8,128)(2,1)} %get-tuple-element.704) | copy-start | bytes 1572868 | tf_op jit(solution)/shard_map/while/body/eval_jaxpr/cond
  71.4 1.9 %copy-start.4 = (bf16[2,256,1,5,128]{4,1,0,3,2:T(8,128)(2,1)S(1)}, bf16[2,256,1,5,128]{4,1,0,3,2:T(8,128)(2,1)}, u32[]{:S(2)}) copy-start(bf16[2,256,1,5,128]{4,1,0,3,2:T(8,128)(2,1)} %get-tuple-element.729) | copy-start | bytes 1966084 | tf_op jit(solution)/shard_map/while/body/eval_jaxpr/cond
  71.4 1.9 %copy-start.8 = (f32[2,1,5,256]{3,2,0,1:T(8,128)S(1)}, f32[2,1,5,256]{3,2,0,1:T(8,128)}, u32[]{:S(2)}) copy-start(f32[2,1,5,256]{3,2,0,1:T(8,128)} %get-tuple-element.727) | copy-start | bytes 30724 | tf_op jit(solution)/shard_map/while/body/eval_jaxpr/cond
  73.2 2.5 %copy-start.6 = (bf16[2048,1,128]{2,0,1:T(8,128)(2,1)S(1)}, bf16[2048,1,128]{2,0,1:T(8,128)(2,1)}, u32[]{:S(2)}) copy-start(bf16[2048,1,128]{2,0,1:T(8,128)(2,1)} %get-tuple-element.728) | copy-start | bytes 1572868 | tf_op jit(solution)/shard_map/while/body/eval_jaxpr/cond
  73.2 2.5 %copy-start.7 = (f32[2,1,5,256]{3,2,0,1:T(8,128)S(1)}, f32[2,1,5,256]{3,2,0,1:T(8,128)}, u32[]{:S(2)}) copy-start(f32[2,1,5,256]{3,2,0,1:T(8,128)} %get-tuple-element.730) | copy-start | bytes 30724 | tf_op jit(solution)/shard_map/while/body/eval_jaxpr/cond
  75.7 3.4 %copy-start.1 = (f32[2048,1,128]{2,0,1:T(8,128)S(1)}, f32[2048,1,128]{2,0,1:T(8,128)}, u32[]{:S(2)}) copy-start(f32[2048,1,128]{2,0,1:T(8,128)} %get-tuple-element.731) | copy-start | bytes 3145732 | tf_op jit(solution)/shard_map/while/body/eval_jaxpr/cond
  80.6 1.0 copy-start.2
  82.4 1.0 copy-start
  83.4 93.4 %reduce-scatter.3.cloned.1.call-start = ((), (), s32[]{:S(2)}) async-start(), calls=%async_computation.5 | async-start | bytes 1179648 | tf_op jit(solution)/shard_map/reduce_scatter | solution.py:167
Sparse Core Ops, SparseCore 0:
  83.5 54.0 reduce-scatter.4
  140.8 35.9 reduce-scatter.2
where the time goes:
time: 186 us; the launch traced here: 185 us
  waiting for transfers between devices  82.3 us (44%)
  blocking collectives  43.5 us (23%)
  matrix products  14.6 us (8%)
  between operations  14.2 us (8%)
  local copies, waits for them, and re-layouts  10 us (5%)
  starting transfers between devices  9.88 us (5%)
  other arithmetic  7.28 us (4%)
  loops' own time  3.42 us (2%)
    reduce_scatter x1, waiting for transfers between devices, layer_pass(): lax.psum_scatter(key_buffer, 'seq', scatter_dimension=0, tiled=True)  37.7 us
    reduce_scatter x1, waiting for transfers between devices, layer_pass(): lax.psum_scatter(value_buffer, 'seq', scatter_dimension=0, tiled=True)  28.6 us
    all_to_all x1, blocking collectives, per_device(): lax.all_to_all(query_final, 'head', split_axis=1, concat_axis=2, tiled=True)  22.6 us
    all_to_all x1, waiting for transfers between devices, per_device(): lax.all_to_all(queries, 'head', split_axis=2, concat_axis=1, tiled=True)  15.3 us
    all_gather x1, blocking collectives, layer_pass(): lax.all_gather(values, 'seq', axis=0, tiled=True)  10.8 us
    all_gather x1, blocking collectives, layer_pass(): lax.all_gather(keys, 'seq', axis=0, tiled=True)  10.1 us
    all_to_all x1, starting transfers between devices, per_device(): lax.all_to_all(queries, 'head', split_axis=2, concat_axis=1, tiled=True)  6.32 us
    unnamed x8, local copies, waits for them, and re-layouts  5.82 us
  transfers between devices with their start and end apart: 4, of which 3 were waited for; matrix products, arithmetic and copies ran while one was open for 4% of the time, Pallas kernels for 0%

commit v1 on v0

v1 whole, which is shorter than its diff:
```python
import functools
import math

import jax
import jax.numpy as jnp
from jax import lax
from jax.experimental import pallas as pl
from jax.experimental.pallas import tpu as pltpu
from jax.sharding import PartitionSpec as P

NEG = -1e30
KEY_BLOCK = 256
VMEM_LIMIT = 56 * 1024 * 1024
SCORE_BYTES = 24 * 1024 * 1024


def exchange(x, seq_count, head_count, flip_seq, flip_head, sends=None):
    pairs = []
    for s in range(seq_count):
        for z in range(head_count):
            if sends is None or sends(s, z):
                pairs.append((s * head_count + z, (s ^ flip_seq) * head_count + (z ^ flip_head)))
    return lax.ppermute(x, ("seq", "head"), pairs)


def attention_kernel(
    column_count,
    head_group,
    info_ref,
    doc_ref,
    doc_rows_ref,
    *refs,
):
    chunk_refs = refs[:4]
    kv_refs = refs[4 : 4 + column_count]
    outs = refs[4 + column_count :]
    dq_refs = outs[:4]
    dkv_refs = outs[4 : 4 + column_count]
    (
        q_rows, g_rows, q_cols, g_cols, keys, values, keys_t,
        e_scr, d_scr, m_scr, max_scr, sum_scr, weight_scr, dqt, dk_acc, dv_acc,
    ) = outs[4 + column_count :]
    layers, group, tokens, width = chunk_refs[0].shape[1:]
    block_tokens = kv_refs[0].shape[2]
    total = keys.shape[0]
    pair = 2 * tokens
    row_count = 2 * pair
    scale = 1.0 / math.sqrt(width)
    exp_scale = scale * math.log2(math.e)
    column = info_ref[0]
    core = info_ref[1]
    z_pair = info_ref[2]
    z_bit = info_ref[3]

    for d in range(column_count):
        for b in range(2):
            start = pl.multiple_of(((column ^ d) * 2 + (core ^ b)) * block_tokens, block_tokens)
            keys[pl.ds(start, block_tokens), :] = kv_refs[d][b, 0]
            values[pl.ds(start, block_tokens), :] = kv_refs[d][b, 1]
    keys_t[...] = keys[...].T
    dk_acc[...] = jnp.zeros_like(dk_acc)
    dv_acc[...] = jnp.zeros_like(dv_acc)

    first = (column * 2 * block_tokens) + z_pair * pair
    second = first + block_tokens
    last = second + pair - 1
    low = doc_ref[first] // KEY_BLOCK
    high = last // KEY_BLOCK + 1
    open_from = doc_ref[last]
    starts, places = [], []
    for begin in (first, second):
        starts.append(doc_rows_ref[pl.ds(begin // pair, 1), :])
        places.append(begin + lax.broadcasted_iota(jnp.int32, (1, pair), 1))
    starts = jnp.concatenate(starts, axis=1)
    places = jnp.concatenate(places, axis=1)

    for layer in range(layers):
        for dz in range(2):
            for dc in range(2):
                at = pl.multiple_of(((core ^ dc) * 2 + (z_bit ^ dz)) * tokens, tokens)
                for h in range(group):
                    q_rows[h, pl.ds(at, tokens), :] = chunk_refs[2 * dz + dc][0, layer, h]
                    g_rows[h, pl.ds(at, tokens), :] = chunk_refs[2 * dz + dc][1, layer, h]
        for h in range(group):
            q_cols[:, pl.ds(h * row_count, row_count)] = q_rows[h].T
            g_cols[:, pl.ds(h * row_count, row_count)] = g_rows[h].T

        for base in range(0, group, head_group):
            heads = range(base, base + head_group)
            lanes = head_group * row_count
            left = base * row_count
            max_scr[...] = jnp.full_like(max_scr, NEG)
            sum_scr[...] = jnp.zeros_like(sum_scr)
            weight_scr[...] = jnp.zeros_like(weight_scr)

            def stats(j, _):
                key_start = pl.multiple_of(j * KEY_BLOCK, KEY_BLOCK)
                rows = pl.ds(key_start, KEY_BLOCK)
                key_block = keys[rows, :]
                value_block = values[rows, :]

                def run(masked):
                    if masked:
                        at = key_start + lax.broadcasted_iota(jnp.int32, (KEY_BLOCK, row_count), 0)
                        allowed = (at >= starts) & (at <= places)
                    for i, h in enumerate(heads):
                        cols = pl.ds(i * row_count, row_count)
                        scores = jnp.dot(
                            key_block, q_cols[:, pl.ds(h * row_count, row_count)],
                            preferred_element_type=jnp.float32,
                        )
                        grads = jnp.dot(
                            value_block, g_cols[:, pl.ds(h * row_count, row_count)],
                            preferred_element_type=jnp.float32,
                        )
                        if masked:
                            scores = jnp.where(allowed, scores, NEG)
                        old = max_scr[:, cols]
                        new = jnp.maximum(old, jnp.max(scores, axis=0, keepdims=True))
                        weights = jnp.exp2((scores - new) * exp_scale)
                        rescale = jnp.exp2((old - new) * exp_scale)
                        max_scr[:, cols] = new
                        m_scr[pl.ds(j, 1), cols] = new
                        sum_scr[:, cols] = sum_scr[:, cols] * rescale + jnp.sum(
                            weights, axis=0, keepdims=True
                        )
                        weight_scr[:, cols] = weight_scr[:, cols] * rescale + jnp.sum(
                            weights * grads, axis=0, keepdims=True
                        )
                        e_scr[rows, cols] = weights
                        d_scr[rows, cols] = grads

                whole = (key_start + KEY_BLOCK - 1 <= first) & (key_start >= open_from)

                @pl.when(whole)
                def _():
                    run(False)

                @pl.when(jnp.logical_not(whole))
                def _():
                    run(True)

                return 0

            lax.fori_loop(low, high, stats, 0)
            inverse = 1.0 / sum_scr[...]
            delta = weight_scr[...] * inverse
            weight_scr[...] = delta
            sum_scr[...] = inverse
            dqt[:, left : left + lanes] = jnp.zeros((width, lanes), jnp.float32)

            def grads_step(j, _):
                key_start = pl.multiple_of(j * KEY_BLOCK, KEY_BLOCK)
                rows = pl.ds(key_start, KEY_BLOCK)
                factor = jnp.exp2((m_scr[pl.ds(j, 1), :] - max_scr[...]) * exp_scale) * sum_scr[...]
                probs_parts, grad_parts = [], []
                for i, h in enumerate(heads):
                    cols = slice(i * row_count, (i + 1) * row_count)
                    probs = e_scr[rows, cols] * factor[:, cols]
                    grad_scores = probs * (d_scr[rows, cols] - weight_scr[:, cols])
                    probs_parts.append(probs.astype(jnp.bfloat16))
                    grad_parts.append(grad_scores.astype(jnp.bfloat16))
                probs_low = jnp.concatenate(probs_parts, axis=1)
                grad_low = jnp.concatenate(grad_parts, axis=1)
                g_all = g_rows[base : base + head_group].reshape(lanes, width)
                q_all = q_rows[base : base + head_group].reshape(lanes, width)
                dv_acc[rows, :] += jnp.dot(probs_low, g_all, preferred_element_type=jnp.float32)
                dk_acc[rows, :] += jnp.dot(grad_low, q_all, preferred_element_type=jnp.float32)
                dqt[:, left : left + lanes] += jnp.dot(
                    keys_t[:, rows], grad_low, preferred_element_type=jnp.float32
                )
                return 0

            lax.fori_loop(low, high, grads_step, 0)

        for h in range(group):
            q_rows[h] = (dqt[:, h * row_count : (h + 1) * row_count] * scale).T.astype(jnp.bfloat16)
        for dz in range(2):
            for dc in range(2):
                at = pl.multiple_of(((core ^ dc) * 2 + (z_bit ^ dz)) * tokens, tokens)
                for h in range(group):
                    dq_refs[2 * dz + dc][layer, h] = q_rows[h, pl.ds(at, tokens), :]

    for d in range(column_count):
        for b in range(2):
            start = pl.multiple_of(((column ^ d) * 2 + (core ^ b)) * block_tokens, block_tokens)
            rows = pl.ds(start, block_tokens)
            dkv_refs[d][b, 0] = (dk_acc[rows, :] * scale).astype(dkv_refs[d].dtype)
            dkv_refs[d][b, 1] = dv_acc[rows, :].astype(dkv_refs[d].dtype)


def attention(info, doc_start, chunks, kv_blocks):
    _, layers, group, tokens, width = chunks[0].shape
    column_count = len(kv_blocks)
    block_tokens = kv_blocks[0].shape[2]
    total = column_count * 2 * block_tokens
    row_count = 4 * tokens
    head_group = group
    while 8 * total * head_group * row_count > SCORE_BYTES:
        head_group = max(k for k in range(1, head_group) if group % k == 0)
    lanes = head_group * row_count
    smem = pl.BlockSpec(memory_space=pltpu.SMEM)
    vmem = pl.BlockSpec(memory_space=pltpu.VMEM)
    f32, bf16 = jnp.float32, jnp.bfloat16
    outs = [jax.ShapeDtypeStruct((layers, group, tokens, width), bf16)] * 4
    outs += [
        jax.ShapeDtypeStruct(kv_blocks[0].shape, f32 if d == 0 else bf16)
        for d in range(column_count)
    ]
    return pl.pallas_call(
        functools.partial(attention_kernel, column_count, head_group),
        out_shape=outs,
        in_specs=[smem, smem] + [vmem] * (1 + 4 + column_count),
        out_specs=[vmem] * len(outs),
        scratch_shapes=[
            pltpu.VMEM((group, row_count, width), bf16),
            pltpu.VMEM((group, row_count, width), bf16),
            pltpu.VMEM((width, group * row_count), bf16),
            pltpu.VMEM((width, group * row_count), bf16),
            pltpu.VMEM((total, width), bf16),
            pltpu.VMEM((total, width), bf16),
            pltpu.VMEM((width, total), bf16),
            pltpu.VMEM((total, lanes), f32),
            pltpu.VMEM((total, lanes), f32),
            pltpu.VMEM((total // KEY_BLOCK, lanes), f32),
            pltpu.VMEM((1, lanes), f32),
            pltpu.VMEM((1, lanes), f32),
            pltpu.VMEM((1, lanes), f32),
            pltpu.VMEM((width, group * row_count), f32),
            pltpu.VMEM((total, width), f32),
            pltpu.VMEM((total, width), f32),
        ],
        compiler_params=pltpu.CompilerParams(vmem_limit_bytes=VMEM_LIMIT),
        name="attention_backward",
    )(info, doc_start, doc_start.reshape(-1, 2 * tokens), *chunks, *kv_blocks)


def per_device(seq_count, head_count, queries, grad_out, keys, values, doc_start):
    layers, tokens, all_heads, width = queries.shape
    key_heads = head_count
    group = all_heads // key_heads
    column_count = seq_count // 2
    swap = functools.partial(exchange, seq_count=seq_count, head_count=head_count)
    s = lax.axis_index("seq")
    z = lax.axis_index("head")
    column, core = s // 2, s % 2
    z_pair, z_bit = z // 2, z % 2
    home = core == z_pair
    info = jnp.stack([column, core, z_pair, z_bit]).astype(jnp.int32)

    own = jnp.stack([keys[:, 0], values[:, 0]])
    from_far = swap(own, flip_seq=0, flip_head=2, sends=lambda s, z: s % 2 == z // 2)
    from_far_core = swap(own, flip_seq=1, flip_head=2, sends=lambda s, z: s % 2 != z // 2)
    from_core = swap(own, flip_seq=1, flip_head=0, sends=lambda s, z: s % 2 != z // 2)
    kv = jnp.stack([jnp.where(home, own, from_far), jnp.where(home, from_core, from_far_core)])
    kv_blocks = [kv] + [swap(kv, flip_seq=2 * d, flip_head=0) for d in range(1, column_count)]

    both = jnp.stack([queries, grad_out]).reshape(2, layers, tokens, 2, 2, group, width)
    both = jnp.transpose(both, (4, 3, 0, 1, 5, 2, 6))

    def piece(dz, dc):
        part = lax.dynamic_index_in_dim(both, z_bit ^ dz, 0, keepdims=False)
        return lax.dynamic_index_in_dim(part, core ^ dc, 0, keepdims=False)

    chunks = [
        piece(0, 0),
        swap(piece(0, 1), flip_seq=1, flip_head=0),
        swap(piece(1, 0), flip_seq=0, flip_head=1),
        swap(piece(1, 1), flip_seq=1, flip_head=1),
    ]
    results = attention(info, doc_start, chunks, kv_blocks)
    dq, dkv = results[:4], results[4:]

    back = [
        dq[0],
        swap(dq[1], flip_seq=1, flip_head=0),
        swap(dq[2], flip_seq=0, flip_head=1),
        swap(dq[3], flip_seq=1, flip_head=1),
    ]
    merged = jnp.stack(back).reshape(2, 2, layers, group, tokens, width)
    merged = jnp.where(z_bit == 1, merged[::-1], merged)
    merged = jnp.where(core == 1, merged[:, ::-1], merged)
    query_grads = jnp.transpose(merged, (2, 4, 1, 0, 3, 5)).reshape(
        layers, tokens, all_heads, width
    )

    mine = dkv[0]
    for d in range(1, column_count):
        mine = mine + swap(dkv[d], flip_seq=2 * d, flip_head=0).astype(jnp.float32)
    low = mine.astype(jnp.bfloat16)
    far = swap(low[0], flip_seq=0, flip_head=2, sends=lambda s, z: s % 2 != z // 2)
    far_core = swap(low[1], flip_seq=1, flip_head=2, sends=lambda s, z: s % 2 != z // 2)
    by_core = swap(low[1], flip_seq=1, flip_head=0, sends=lambda s, z: s % 2 == z // 2)
    near = jnp.where(home, mine[0], by_core.astype(jnp.float32))
    final = near + jnp.where(home, far, far_core).astype(jnp.float32)
    final = final.astype(jnp.bfloat16)[:, :, None, :]
    return query_grads, final[0], final[1]


def solution(mesh):
    tokens_spec = P(None, ("seq", "head"), None, None)
    keys_spec = P("seq", "head", None)
    return jax.shard_map(
        functools.partial(per_device, mesh.shape["seq"], mesh.shape["head"]),
        mesh=mesh,
        in_specs=(tokens_spec, tokens_spec, keys_spec, keys_spec, P()),
        out_specs=(tokens_spec, keys_spec, keys_spec),
        check_vma=False,
    )
```

time: 186 us -> 87.8 us (0.47)
  waiting for transfers between devices: 82.3 us -> 27.7 us
  blocking collectives: 43.5 us -> 0 us
  starting transfers between devices: 9.88 us -> 42.8 us
  matrix products: 14.6 us -> 0 us
  between operations: 14.2 us -> 0.93 us
  Pallas kernels: 0 us -> 9.37 us
  local copies, waits for them, and re-layouts: 10 us -> 2.3 us
  loops' own time: 3.42 us -> 0 us
  other arithmetic: 7.28 us -> 5.35 us
    reduce_scatter x2 -> x0, waiting for transfers between devices: 66.3 us -> none  [the longest x1 37.7 us: layer_pass(): lax.psum_scatter(key_buffer, 'seq', scatter_dimension=0, tiled=True)]
    ppermute x0 -> x18, starting transfers between devices: none -> 42.8 us  [exchange(): return lax.ppermute(x, ('seq', 'head'), pairs)]
    ppermute x0 -> x18, waiting for transfers between devices: none -> 27.7 us  [exchange(): return lax.ppermute(x, ('seq', 'head'), pairs)]
    all_to_all x1 -> x0, blocking collectives: 22.6 us -> none  [per_device(): lax.all_to_all(query_final, 'head', split_axis=1, concat_axis=2, tiled=True)]
    all_gather x2 -> x0, blocking collectives: 20.9 us -> none  [the longest x1 10.8 us: layer_pass(): lax.all_gather(values, 'seq', axis=0, tiled=True)]
    all_to_all x2 -> x0, waiting for transfers between devices: 15.3 us -> none  [the longest x1 15.3 us: per_device(): lax.all_to_all(queries, 'head', split_axis=2, concat_axis=1, tiled=True)]
    dot_general x7 -> x0, matrix products: 14.6 us -> none  [the longest x1 3.34 us: grads_compute(): jnp.einsum('lrkgd,nkd->lkgrn', group[1], value_block, preferred_element_t...]
    all_to_all x2 -> x0, starting transfers between devices: 9.8 us -> none  [the longest x1 6.32 us: per_device(): lax.all_to_all(queries, 'head', split_axis=2, concat_axis=1, tiled=True)]
  transfers between devices with their start and end apart: 4 -> 18, of which waited for: 3 -> 6; matrix products, arithmetic and copies ran while one was open for 4% -> 6% of each run, Pallas kernels for 0% -> 0%
where the time goes in v1:
time: 87.8 us; the launch traced here: 88.5 us
  starting transfers between devices  42.8 us (49%)
  waiting for transfers between devices  27.7 us (32%)
  Pallas kernels  9.37 us (11%)
  other arithmetic  5.35 us (6%)
  local copies, waits for them, and re-layouts  2.3 us (3%)
  between operations  0.93 us (1%)
    ppermute x18, starting transfers between devices, exchange(): return lax.ppermute(x, ('seq', 'head'), pairs)  42.8 us
    ppermute x18, waiting for transfers between devices, exchange(): return lax.ppermute(x, ('seq', 'head'), pairs)  27.7 us
    pallas_call x1, Pallas kernels, attention(): pl.pallas_call(functools.partial(attention_kernel, column_count, head_gro...  9.37 us
    squeeze x1, other arithmetic, piece(): return lax.dynamic_index_in_dim(part, core ^ dc, 0, keepdims=False)  2.27 us
  transfers between devices with their start and end apart: 18, of which 6 were waited for; matrix products, arithmetic and copies ran while one was open for 6% of the time, Pallas kernels for 0%

profile of v1, /device:TPU:0, one launch (start us, length us, event | category | flops | bytes accessed | tf_op | source)
XLA Modules:
  0.0 88.5 jit_solution(16102690455605165157)
XLA Ops:
  0.6 0.9 %pad_maximum_fusion.2 = bf16[2,256,128]{2,1,0:T(8,128)(2,1)S(1)} fusion(bf16[1,256,128]{2,1,0:T(8,128)(2,1)} %bitcast.65, bf16[1,256,128]{2,1,0:T(8,128)(2,1)} %bitcast.67), kind=kLoop, calls=%fused_computation.28 | loop fusion | flops 65536 | bytes 262144 | tf_op jit(solution)/shard_map/stack | solution.py:251
  1.5 1.3 %collective-permute-start.4 = (bf16[2,256,128]{2,1,0:T(8,128)(2,1)S(1)}, bf16[2,256,128]{2,1,0:T(8,128)(2,1)S(1)}, u32[]{:S(2)}, u32[]{:S(2)}) collective-permute-start(bf16[2,256,128]{2,1,0:T(8,128)(2,1)S(1)} %pad_maximum_fusion.2), channel_id=1, source_target_pairs={{2,6},{3,7},{4,0},{5,1},{10,14},{11,15},{12,8},{13,9},{18,22},{19,... | collective-permute-start | bytes 393224 | tf_op jit(solution)/shard_map/ppermute | solution.py:23
  2.8 0.7 collective-permute-start.5
  3.5 7.7 %collective-permute-start.3 = (bf16[2,256,128]{2,1,0:T(8,128)(2,1)S(1)}, bf16[2,256,128]{2,1,0:T(8,128)(2,1)S(1)}, u32[]{:S(2)}, u32[]{:S(2)}) collective-permute-start(bf16[2,256,128]{2,1,0:T(8,128)(2,1)S(1)} %pad_maximum_fusion.2), channel_id=1, source_target_pairs={{0,2},{1,3},{6,4},{7,5},{8,10},{9,11},{14,12},{15,13},{16,18},{17,... | collective-permute-start | bytes 393224 | tf_op jit(solution)/shard_map/ppermute | solution.py:23
  11.2 0.0 copy-start.5
  11.2 0.0 copy-start.6
  11.2 2.3 %fusion.2 = (bf16[2,2,5,64,128]{4,3,2,1,0:T(8,128)(2,1)S(1)}, bf16[2,2,5,64,128]{4,3,2,1,0:T(8,128)(2,1)}, bf16[2,2,5,64,128]{4,3,2,1,0:T(8,128)(2,1)S(1)}, bf16[2,2,5,64,128]{4,3,2,1,0:T(8,128)(2,1)S(1)}) fusion(s32[]{:T(128)S(6)} %select_n.91, s32[]{:T(128)S(6)} %select_n.93, bf16[1,2,64,2,2,5,128]{6,2,5,4,3,1,0:T(8,128)(2,1)} %bitcast.63, ...), kind=kLoop, calls=%fused_computation.14 | loop fusion | flops 655360 | bytes 2621456 | tf_op jit(solution)/shard_map/jit(dynamic_index_in_dim)/squeeze | solution.py:263
  13.5 0.7 collective-permute-start.2
  14.2 1.5 %collective-permute-start.1 = (bf16[2,2,5,64,128]{4,3,2,1,0:T(8,128)(2,1)S(1)}, bf16[2,2,5,64,128]{4,3,2,1,0:T(8,128)(2,1)S(1)}, u32[]{:S(2)}, u32[]{:S(2)}) collective-permute-start(bf16[2,2,5,64,128]{4,3,2,1,0:T(8,128)(2,1)S(1)} %get-tuple-element.23), channel_id=1, source_target_pairs={{0,1},{1,0},{2,3},{3,2},{4,5},{5,4},{6,7},{7,6},{8,9},{9,8},{10,11... | collective-permute-start | bytes 983048 | tf_op jit(solution)/shard_map/ppermute | solution.py:23
  15.7 0.0 collective-permute-done.4
  15.7 0.1 collective-permute-start
  15.8 0.0 collective-permute-done.5
  15.8 0.0 collective-permute-done.3
  15.8 0.0 copy-done.5
  15.9 0.0 copy-done.6
  15.9 0.0 copy-start
  15.9 2.7 %collective-permute-start.8 = (bf16[2,2,256,128]{3,2,1,0:T(8,128)(2,1)S(1)}, bf16[2,2,256,128]{3,2,1,0:T(8,128)(2,1)S(1)}, u32[]{:S(2)}, u32[]{:S(2)}) collective-permute-start(bf16[2,2,256,128]{3,2,1,0:T(8,128)(2,1)S(1)} %pad_maximum_fusion.1.refs_4_), channel_id=1, source_target_pairs={{0,24},{1,25},{2,26},{3,27},{4,28},{5,29},{6,30},{7,31},{8,16},{9,... | collective-permute-start | bytes 786440 | tf_op jit(solution)/shard_map/ppermute | solution.py:23
  18.6 0.5 collective-permute-start.7
  19.1 4.0 %collective-permute-done.2.refs_3_ = bf16[2,2,5,64,128]{4,3,2,1,0:T(8,128)(2,1)S(1)} collective-permute-done((bf16[2,2,5,64,128]{4,3,2,1,0:T(8,128)(2,1)S(1)}, bf16[2,2,5,64,128]{4,3,2,1,0:T(8,128)(2,1)S(1)}, u32[]{:S(2)}, u32[]{:S(2)}) %collective-permute-start.2) | collective-permute-done | bytes 327712 | tf_op jit(solution)/shard_map/ppermute | solution.py:23
  23.1 0.0 copy-start.2
  23.1 2.7 %collective-permute-start.6 = (bf16[2,2,256,128]{3,2,1,0:T(8,128)(2,1)S(1)}, bf16[2,2,256,128]{3,2,1,0:T(8,128)(2,1)S(1)}, u32[]{:S(2)}, u32[]{:S(2)}) collective-permute-start(bf16[2,2,256,128]{3,2,1,0:T(8,128)(2,1)S(1)} %pad_maximum_fusion.1.refs_4_), channel_id=1, source_target_pairs={{0,8},{1,9},{2,10},{3,11},{4,12},{5,13},{6,14},{7,15},{8,0},{9,1},... | collective-permute-start | bytes 786440 | tf_op jit(solution)/shard_map/ppermute | solution.py:23
  25.8 0.6 pad_add_fusion.info_ref
  26.4 4.5 %collective-permute-done.1.refs_2_ = bf16[2,2,5,64,128]{4,3,2,1,0:T(8,128)(2,1)S(1)} collective-permute-done((bf16[2,2,5,64,128]{4,3,2,1,0:T(8,128)(2,1)S(1)}, bf16[2,2,5,64,128]{4,3,2,1,0:T(8,128)(2,1)S(1)}, u32[]{:S(2)}, u32[]{:S(2)}) %collective-permute-start.1) | collective-permute-done | bytes 327712 | tf_op jit(solution)/shard_map/ppermute | solution.py:23
  30.8 0.0 copy-start.3
  30.8 0.0 collective-permute-done.refs_1_
  30.8 0.0 collective-permute-done.8.refs_7_
  30.8 0.0 copy-start.7
  30.9 0.8 collective-permute-done.7.refs_6_
  31.7 1.1 %collective-permute-done.6.refs_5_ = bf16[2,2,256,128]{3,2,1,0:T(8,128)(2,1)S(1)} collective-permute-done((bf16[2,2,256,128]{3,2,1,0:T(8,128)(2,1)S(1)}, bf16[2,2,256,128]{3,2,1,0:T(8,128)(2,1)S(1)}, u32[]{:S(2)}, u32[]{:S(2)}) %collective-permute-start.6) | collective-permute-done | bytes 262176 | tf_op jit(solution)/shard_map/ppermute | solution.py:23
  32.8 0.0 copy-done
  32.8 0.0 copy-done.2
  32.8 0.0 copy-done.3
  32.8 0.0 copy-done.4
  32.9 0.0 copy-done.7
  32.9 0.0 copy-done.8
  32.9 0.7 copy-done.9
  33.6 9.4 %attention_backward.1 = (bf16[2,5,64,128]{3,2,1,0:T(8,128)(2,1)}, bf16[2,5,64,128]{3,2,1,0:T(8,128)(2,1)}, bf16[2,5,64,128]{3,2,1,0:T(8,128)(2,1)}, bf16[2,5,64,...) custom-call(s32[4]{0:T(128)} %pad_add_fusion.info_ref, ...), custom_call_target="tpu_custom_call" | custom-call | tf_op jit(solution)/shard_map/attention_backward/pallas_call | solution.py:210
  42.9 0.0 collective-permute-start.9
  42.9 0.1 collective-permute-start.10
  43.0 1.8 %collective-permute-start.11 = (bf16[2,5,64,128]{3,2,1,0:T(8,128)(2,1)}, bf16[2,5,64,128]{3,2,1,0:T(8,128)(2,1)S(1)}, u32[]{:S(2)}, u32[]{:S(2)}) collective-permute-start(bf16[2,5,64,128]{3,2,1,0:T(8,128)(2,1)} %get-tuple-element.14), channel_id=1, source_target_pairs={{0,5},{1,4},{2,7},{3,6},{4,1},{5,0},{6,3},{7,2},{8,13},{9,12},{10,... | collective-permute-start | bytes 491528 | tf_op jit(solution)/shard_map/ppermute | solution.py:23
  44.8 6.6 %collective-permute-start.12 = (bf16[2,2,256,128]{3,2,1,0:T(8,128)(2,1)}, bf16[2,2,256,128]{3,2,1,0:T(8,128)(2,1)S(1)}, u32[]{:S(2)}, u32[]{:S(2)}) collective-permute-start(bf16[2,2,256,128]{3,2,1,0:T(8,128)(2,1)} %get-tuple-element.16), channel_id=1, source_target_pairs={{0,8},{1,9},{2,10},{3,11},{4,12},{5,13},{6,14},{7,15},{8,0},{9,1},... | collective-permute-start | bytes 786440 | tf_op jit(solution)/shard_map/ppermute | solution.py:23
  51.4 11.9 %collective-permute-start.13 = (bf16[2,2,256,128]{3,2,1,0:T(8,128)(2,1)}, bf16[2,2,256,128]{3,2,1,0:T(8,128)(2,1)S(1)}, u32[]{:S(2)}, u32[]{:S(2)}) collective-permute-start(bf16[2,2,256,128]{3,2,1,0:T(8,128)(2,1)} %get-tuple-element.17), channel_id=1, source_target_pairs={{0,16},{1,17},{2,18},{3,19},{4,20},{5,21},{6,22},{7,23},{8,24},{9,... | collective-permute-start | bytes 786440 | tf_op jit(solution)/shard_map/ppermute | solution.py:23
  63.3 0.0 collective-permute-done.9
  63.3 0.0 collective-permute-start.14
  63.3 0.0 collective-permute-done.10
  63.3 0.0 collective-permute-done.11
  63.3 1.0 %pad_maximum_fusion = bf16[4,2,5,64,128]{4,3,2,1,0:T(8,128)(2,1)S(1)} fusion(bf16[1,2,5,64,128]{4,3,2,1,0:T(8,128)(2,1)S(1)} %bitcast.72, bf16[1,2,5,64,128]{4,3,2,1,0:T(8,128)(2,1)S(1)} %bitcast.71, bf16[1,2,5,64,128]{4,3,2,1,0:T(8,128)(2,1)S(1)} %bitcast.70, bf16[1,2,5,64,128]{4,3,2,1,0:T(8,128)(2,1)} %bitcast.69), kind=kLoop, calls=%fused_computation.11 | loop fusion | flops 983040 | bytes 1310720 | tf_op jit(solution)/shard_map/stack | solution.py:280
  64.3 0.0 copy-start.1
  64.3 0.2 reverse_select_fusion.1
  64.5 0.0 collective-permute-done.12
  64.5 11.1 %collective-permute-done.13 = bf16[2,2,256,128]{3,2,1,0:T(8,128)(2,1)S(1)} collective-permute-done((bf16[2,2,256,128]{3,2,1,0:T(8,128)(2,1)}, bf16[2,2,256,128]{3,2,1,0:T(8,128)(2,1)S(1)}, u32[]{:S(2)}, u32[]{:S(2)}) %collective-permute-start.13) | collective-permute-done | bytes 262176 | tf_op jit(solution)/shard_map/ppermute | solution.py:23
  75.7 0.0 collective-permute-done.14
  75.7 0.0 copy-done.1
  75.7 0.1 fusion.12
  75.8 0.7 collective-permute-start.17
  76.5 2.7 %collective-permute-start.15 = (bf16[2,256,128]{2,1,0:T(8,128)(2,1)S(1)}, bf16[2,256,128]{2,1,0:T(8,128)(2,1)S(1)}, u32[]{:S(2)}, u32[]{:S(2)}) collective-permute-start(bf16[2,256,128]{2,1,0:T(8,128)(2,1)S(1)} %get-tuple-element.26), channel_id=1, source_target_pairs={{0,4},{1,5},{6,2},{7,3},{8,12},{9,13},{14,10},{15,11},{16,20},{17,... | collective-permute-start | bytes 393224 | tf_op jit(solution)/shard_map/ppermute | solution.py:23
  79.2 1.3 %collective-permute-start.16 = (bf16[2,256,128]{2,1,0:T(8,128)(2,1)S(1)}, bf16[2,256,128]{2,1,0:T(8,128)(2,1)S(1)}, u32[]{:S(2)}, u32[]{:S(2)}) collective-permute-start(bf16[2,256,128]{2,1,0:T(8,128)(2,1)S(1)} %get-tuple-element.25), channel_id=1, source_target_pairs={{2,0},{3,1},{4,6},{5,7},{10,8},{11,9},{12,14},{13,15},{18,16},{19,... | collective-permute-start | bytes 393224 | tf_op jit(solution)/shard_map/ppermute | solution.py:23
  80.5 0.2 fusion
  80.7 0.9 %copy.11 = bf16[2,64,2,2,5,128]{5,1,4,3,2,0:T(8,128)(2,1)} copy(bf16[2,64,2,2,5,128]{5,1,4,0,2,3:T(8,128)(2,1)S(1)} %fusion) | data formatting | bytes 1310720 | tf_op jit(solution)/shard_map/transpose | solution.py:283
  81.6 6.2 %collective-permute-done.16 = bf16[2,256,128]{2,1,0:T(8,128)(2,1)S(1)} collective-permute-done((bf16[2,256,128]{2,1,0:T(8,128)(2,1)S(1)}, bf16[2,256,128]{2,1,0:T(8,128)(2,1)S(1)}, u32[]{:S(2)}, u32[]{:S(2)}) %collective-permute-start.16) | collective-permute-done | bytes 131104 | tf_op jit(solution)/shard_map/ppermute | solution.py:23
  87.8 0.0 collective-permute-done.17
  87.8 0.0 collective-permute-done.15
  87.8 0.1 fusion.11
  87.8 0.7 slice_bitcast_fusion.3
  (7 shorter events, 0.1 us)
Async XLA Ops:
  1.5 14.2 %collective-permute-start.4 = (bf16[2,256,128]{2,1,0:T(8,128)(2,1)S(1)}, bf16[2,256,128]{2,1,0:T(8,128)(2,1)S(1)}, u32[]{:S(2)}, u32[]{:S(2)}) collective-permute-start(bf16[2,256,128]{2,1,0:T(8,128)(2,1)S(1)} %pad_maximum_fusion.2), channel_id=1, source_target_pairs={{2,6},{3,7},{4,0},{5,1},{10,14},{11,15},{12,8},{13,9},{18,22},{19,... | collective-permute-start | bytes 393224 | tf_op jit(solution)/shard_map/ppermute | solution.py:23
  2.8 13.0 %collective-permute-start.5 = (bf16[2,256,128]{2,1,0:T(8,128)(2,1)S(1)}, bf16[2,256,128]{2,1,0:T(8,128)(2,1)S(1)}, u32[]{:S(2)}, u32[]{:S(2)}) collective-permute-start(bf16[2,256,128]{2,1,0:T(8,128)(2,1)S(1)} %pad_maximum_fusion.2), channel_id=1, source_target_pairs={{2,4},{3,5},{4,2},{5,3},{10,12},{11,13},{12,10},{13,11},{18,20},{1... | collective-permute-start | bytes 393224 | tf_op jit(solution)/shard_map/ppermute | solution.py:23
  3.5 12.3 %collective-permute-start.3 = (bf16[2,256,128]{2,1,0:T(8,128)(2,1)S(1)}, bf16[2,256,128]{2,1,0:T(8,128)(2,1)S(1)}, u32[]{:S(2)}, u32[]{:S(2)}) collective-permute-start(bf16[2,256,128]{2,1,0:T(8,128)(2,1)S(1)} %pad_maximum_fusion.2), channel_id=1, source_target_pairs={{0,2},{1,3},{6,4},{7,5},{8,10},{9,11},{14,12},{15,13},{16,18},{17,... | collective-permute-start | bytes 393224 | tf_op jit(solution)/shard_map/ppermute | solution.py:23
  11.2 4.6 %copy-start.5 = (bf16[256,1,128]{2,0,1:T(8,128)(2,1)S(1)}, bf16[256,1,128]{2,0,1:T(8,128)(2,1)}, u32[]{:S(2)}) copy-start(bf16[256,1,128]{2,0,1:T(8,128)(2,1)} %param.8) | copy-start | bytes 196612
  11.2 4.6 %copy-start.6 = (bf16[256,1,128]{2,0,1:T(8,128)(2,1)S(1)}, bf16[256,1,128]{2,0,1:T(8,128)(2,1)}, u32[]{:S(2)}) copy-start(bf16[256,1,128]{2,0,1:T(8,128)(2,1)} %param.7) | copy-start | bytes 196612
  13.5 9.6 %collective-permute-start.2 = (bf16[2,2,5,64,128]{4,3,2,1,0:T(8,128)(2,1)S(1)}, bf16[2,2,5,64,128]{4,3,2,1,0:T(8,128)(2,1)S(1)}, u32[]{:S(2)}, u32[]{:S(2)}) collective-permute-start(bf16[2,2,5,64,128]{4,3,2,1,0:T(8,128)(2,1)S(1)} %get-tuple-element.21), channel_id=1, source_target_pairs={{0,5},{1,4},{2,7},{3,6},{4,1},{5,0},{6,3},{7,2},{8,13},{9,12},{10,... | collective-permute-start | bytes 983048 | tf_op jit(solution)/shard_map/ppermute | solution.py:23
  14.2 16.7 %collective-permute-start.1 = (bf16[2,2,5,64,128]{4,3,2,1,0:T(8,128)(2,1)S(1)}, bf16[2,2,5,64,128]{4,3,2,1,0:T(8,128)(2,1)S(1)}, u32[]{:S(2)}, u32[]{:S(2)}) collective-permute-start(bf16[2,2,5,64,128]{4,3,2,1,0:T(8,128)(2,1)S(1)} %get-tuple-element.23), channel_id=1, source_target_pairs={{0,1},{1,0},{2,3},{3,2},{4,5},{5,4},{6,7},{7,6},{8,9},{9,8},{10,11... | collective-permute-start | bytes 983048 | tf_op jit(solution)/shard_map/ppermute | solution.py:23
  15.7 15.1 %collective-permute-start = (bf16[2,2,5,64,128]{4,3,2,1,0:T(8,128)(2,1)S(1)}, bf16[2,2,5,64,128]{4,3,2,1,0:T(8,128)(2,1)S(1)}, u32[]{:S(2)}, u32[]{:S(2)}) collective-permute-start(bf16[2,2,5,64,128]{4,3,2,1,0:T(8,128)(2,1)S(1)} %get-tuple-element.24), channel_id=1, source_target_pairs={{0,4},{1,5},{2,6},{3,7},{4,0},{5,1},{6,2},{7,3},{8,12},{9,13},{10,... | collective-permute-start | bytes 983048 | tf_op jit(solution)/shard_map/ppermute | solution.py:23
  15.9 16.9 %copy-start = (bf16[2,2,256,128]{3,2,1,0:T(8,128)(2,1)}, bf16[2,2,256,128]{3,2,1,0:T(8,128)(2,1)S(1)}, u32[]{:S(2)}) copy-start(bf16[2,2,256,128]{3,2,1,0:T(8,128)(2,1)S(1)} %pad_maximum_fusion.1.refs_4_) | copy-start | bytes 786436
  15.9 14.9 %collective-permute-start.8 = (bf16[2,2,256,128]{3,2,1,0:T(8,128)(2,1)S(1)}, bf16[2,2,256,128]{3,2,1,0:T(8,128)(2,1)S(1)}, u32[]{:S(2)}, u32[]{:S(2)}) collective-permute-start(bf16[2,2,256,128]{3,2,1,0:T(8,128)(2,1)S(1)} %pad_maximum_fusion.1.refs_4_), channel_id=1, source_target_pairs={{0,24},{1,25},{2,26},{3,27},{4,28},{5,29},{6,30},{7,31},{8,16},{9,... | collective-permute-start | bytes 786440 | tf_op jit(solution)/shard_map/ppermute | solution.py:23
  18.6 13.1 %collective-permute-start.7 = (bf16[2,2,256,128]{3,2,1,0:T(8,128)(2,1)S(1)}, bf16[2,2,256,128]{3,2,1,0:T(8,128)(2,1)S(1)}, u32[]{:S(2)}, u32[]{:S(2)}) collective-permute-start(bf16[2,2,256,128]{3,2,1,0:T(8,128)(2,1)S(1)} %pad_maximum_fusion.1.refs_4_), channel_id=1, source_target_pairs={{0,16},{1,17},{2,18},{3,19},{4,20},{5,21},{6,22},{7,23},{8,24},{9,... | collective-permute-start | bytes 786440 | tf_op jit(solution)/shard_map/ppermute | solution.py:23
  23.1 9.7 %copy-start.2 = (bf16[2,2,5,64,128]{4,3,2,1,0:T(8,128)(2,1)}, bf16[2,2,5,64,128]{4,3,2,1,0:T(8,128)(2,1)S(1)}, u32[]{:S(2)}) copy-start(bf16[2,2,5,64,128]{4,3,2,1,0:T(8,128)(2,1)S(1)} %collective-permute-done.2.refs_3_) | copy-start | bytes 983044
  23.1 9.7 %collective-permute-start.6 = (bf16[2,2,256,128]{3,2,1,0:T(8,128)(2,1)S(1)}, bf16[2,2,256,128]{3,2,1,0:T(8,128)(2,1)S(1)}, u32[]{:S(2)}, u32[]{:S(2)}) collective-permute-start(bf16[2,2,256,128]{3,2,1,0:T(8,128)(2,1)S(1)} %pad_maximum_fusion.1.refs_4_), channel_id=1, source_target_pairs={{0,8},{1,9},{2,10},{3,11},{4,12},{5,13},{6,14},{7,15},{8,0},{9,1},... | collective-permute-start | bytes 786440 | tf_op jit(solution)/shard_map/ppermute | solution.py:23
  30.8 2.0 %copy-start.3 = (bf16[2,2,5,64,128]{4,3,2,1,0:T(8,128)(2,1)}, bf16[2,2,5,64,128]{4,3,2,1,0:T(8,128)(2,1)S(1)}, u32[]{:S(2)}) copy-start(bf16[2,2,5,64,128]{4,3,2,1,0:T(8,128)(2,1)S(1)} %collective-permute-done.1.refs_2_) | copy-start | bytes 983044
  30.8 2.0 %copy-start.4 = (bf16[2,2,5,64,128]{4,3,2,1,0:T(8,128)(2,1)}, bf16[2,2,5,64,128]{4,3,2,1,0:T(8,128)(2,1)S(1)}, u32[]{:S(2)}) copy-start(bf16[2,2,5,64,128]{4,3,2,1,0:T(8,128)(2,1)S(1)} %collective-permute-done.refs_1_) | copy-start | bytes 983044
  30.8 2.0 %copy-start.7 = (bf16[2,2,256,128]{3,2,1,0:T(8,128)(2,1)}, bf16[2,2,256,128]{3,2,1,0:T(8,128)(2,1)S(1)}, u32[]{:S(2)}) copy-start(bf16[2,2,256,128]{3,2,1,0:T(8,128)(2,1)S(1)} %collective-permute-done.8.refs_7_) | copy-start | bytes 786436
  31.7 1.2 %copy-start.8 = (bf16[2,2,256,128]{3,2,1,0:T(8,128)(2,1)}, bf16[2,2,256,128]{3,2,1,0:T(8,128)(2,1)S(1)}, u32[]{:S(2)}) copy-start(bf16[2,2,256,128]{3,2,1,0:T(8,128)(2,1)S(1)} %collective-permute-done.7.refs_6_) | copy-start | bytes 786436
  32.8 0.7 copy-start.9
  42.9 20.4 %collective-permute-start.9 = (bf16[2,5,64,128]{3,2,1,0:T(8,128)(2,1)}, bf16[2,5,64,128]{3,2,1,0:T(8,128)(2,1)S(1)}, u32[]{:S(2)}, u32[]{:S(2)}) collective-permute-start(bf16[2,5,64,128]{3,2,1,0:T(8,128)(2,1)} %get-tuple-element.12), channel_id=1, source_target_pairs={{0,4},{1,5},{2,6},{3,7},{4,0},{5,1},{6,2},{7,3},{8,12},{9,13},{10,... | collective-permute-start | bytes 491528 | tf_op jit(solution)/shard_map/ppermute | solution.py:23
  42.9 20.4 %collective-permute-start.10 = (bf16[2,5,64,128]{3,2,1,0:T(8,128)(2,1)}, bf16[2,5,64,128]{3,2,1,0:T(8,128)(2,1)S(1)}, u32[]{:S(2)}, u32[]{:S(2)}) collective-permute-start(bf16[2,5,64,128]{3,2,1,0:T(8,128)(2,1)} %get-tuple-element.13), channel_id=1, source_target_pairs={{0,1},{1,0},{2,3},{3,2},{4,5},{5,4},{6,7},{7,6},{8,9},{9,8},{10,11... | collective-permute-start | bytes 491528 | tf_op jit(solution)/shard_map/ppermute | solution.py:23
  43.0 20.3 %collective-permute-start.11 = (bf16[2,5,64,128]{3,2,1,0:T(8,128)(2,1)}, bf16[2,5,64,128]{3,2,1,0:T(8,128)(2,1)S(1)}, u32[]{:S(2)}, u32[]{:S(2)}) collective-permute-start(bf16[2,5,64,128]{3,2,1,0:T(8,128)(2,1)} %get-tuple-element.14), channel_id=1, source_target_pairs={{0,5},{1,4},{2,7},{3,6},{4,1},{5,0},{6,3},{7,2},{8,13},{9,12},{10,... | collective-permute-start | bytes 491528 | tf_op jit(solution)/shard_map/ppermute | solution.py:23
  44.8 19.7 %collective-permute-start.12 = (bf16[2,2,256,128]{3,2,1,0:T(8,128)(2,1)}, bf16[2,2,256,128]{3,2,1,0:T(8,128)(2,1)S(1)}, u32[]{:S(2)}, u32[]{:S(2)}) collective-permute-start(bf16[2,2,256,128]{3,2,1,0:T(8,128)(2,1)} %get-tuple-element.16), channel_id=1, source_target_pairs={{0,8},{1,9},{2,10},{3,11},{4,12},{5,13},{6,14},{7,15},{8,0},{9,1},... | collective-permute-start | bytes 786440 | tf_op jit(solution)/shard_map/ppermute | solution.py:23
  51.4 24.3 %collective-permute-start.13 = (bf16[2,2,256,128]{3,2,1,0:T(8,128)(2,1)}, bf16[2,2,256,128]{3,2,1,0:T(8,128)(2,1)S(1)}, u32[]{:S(2)}, u32[]{:S(2)}) collective-permute-start(bf16[2,2,256,128]{3,2,1,0:T(8,128)(2,1)} %get-tuple-element.17), channel_id=1, source_target_pairs={{0,16},{1,17},{2,18},{3,19},{4,20},{5,21},{6,22},{7,23},{8,24},{9,... | collective-permute-start | bytes 786440 | tf_op jit(solution)/shard_map/ppermute | solution.py:23
  63.3 12.4 %collective-permute-start.14 = (bf16[2,2,256,128]{3,2,1,0:T(8,128)(2,1)}, bf16[2,2,256,128]{3,2,1,0:T(8,128)(2,1)S(1)}, u32[]{:S(2)}, u32[]{:S(2)}) collective-permute-start(bf16[2,2,256,128]{3,2,1,0:T(8,128)(2,1)} %get-tuple-element.18), channel_id=1, source_target_pairs={{0,24},{1,25},{2,26},{3,27},{4,28},{5,29},{6,30},{7,31},{8,16},{9,... | collective-permute-start | bytes 786440 | tf_op jit(solution)/shard_map/ppermute | solution.py:23
  64.3 11.3 %copy-start.1 = (f32[2,2,256,128]{3,2,1,0:T(8,128)S(1)}, f32[2,2,256,128]{3,2,1,0:T(8,128)}, u32[]{:S(2)}) copy-start(f32[2,2,256,128]{3,2,1,0:T(8,128)} %get-tuple-element.15) | copy-start | bytes 1572868
  75.8 11.9 %collective-permute-start.17 = (bf16[2,256,128]{2,1,0:T(8,128)(2,1)S(1)}, bf16[2,256,128]{2,1,0:T(8,128)(2,1)S(1)}, u32[]{:S(2)}, u32[]{:S(2)}) collective-permute-start(bf16[2,256,128]{2,1,0:T(8,128)(2,1)S(1)} %get-tuple-element.26), channel_id=1, source_target_pairs={{2,4},{3,5},{4,2},{5,3},{10,12},{11,13},{12,10},{13,11},{18,20},{1... | collective-permute-start | bytes 393224 | tf_op jit(solution)/shard_map/ppermute | solution.py:23
  76.5 11.3 %collective-permute-start.15 = (bf16[2,256,128]{2,1,0:T(8,128)(2,1)S(1)}, bf16[2,256,128]{2,1,0:T(8,128)(2,1)S(1)}, u32[]{:S(2)}, u32[]{:S(2)}) collective-permute-start(bf16[2,256,128]{2,1,0:T(8,128)(2,1)S(1)} %get-tuple-element.26), channel_id=1, source_target_pairs={{0,4},{1,5},{6,2},{7,3},{8,12},{9,13},{14,10},{15,11},{16,20},{17,... | collective-permute-start | bytes 393224 | tf_op jit(solution)/shard_map/ppermute | solution.py:23
  79.2 8.5 %collective-permute-start.16 = (bf16[2,256,128]{2,1,0:T(8,128)(2,1)S(1)}, bf16[2,256,128]{2,1,0:T(8,128)(2,1)S(1)}, u32[]{:S(2)}, u32[]{:S(2)}) collective-permute-start(bf16[2,256,128]{2,1,0:T(8,128)(2,1)S(1)} %get-tuple-element.25), channel_id=1, source_target_pairs={{2,0},{3,1},{4,6},{5,7},{10,8},{11,9},{12,14},{13,15},{18,16},{19,... | collective-permute-start | bytes 393224 | tf_op jit(solution)/shard_map/ppermute | solution.py:23
